TPU v7x, 32 devices: a whole 2x2x4 slice. The times are simulated.
32 devices in a mesh: seq: 16 (over z, x, core), mp: 2 (over y).
Axes of the slice: x: 2, y: 2, z: 4, core: 2. Of those that a mesh axis runs over, the one named last changes fastest.
Arguments:
- queries: bfloat16 [2048, 2048], P('seq', 'mp'), may hold values from -200 to 200
- keys: bfloat16 [2048, 256], P('seq', 'mp'), may hold values from -7 to 7
- values: float32 [2048, 256], P('seq', 'mp'), may hold values from -24 to 24
- inputs_x: bfloat16 [2048, 2048], P('seq', 'mp'), may hold values from -6 to 6
- in_b: bfloat16 [2048, 128], P('seq'), may hold values from -6 to 6
- in_c: bfloat16 [2048, 128], P('seq'), may hold values from -6 to 6
- log_decay: float32 [2048, 16], P('seq', 'mp'), may hold values from -2 to 0
Outputs:
- grad_x: float32 [2048, 2048], P('seq', 'mp')
- grad_b: float32 [2048, 128], P(('seq', 'mp'))
- grad_c: float32 [2048, 128], P(('seq', 'mp'))
All inputs are finite; a program needn't handle non-finite values.
Results may differ from a plain program's by a relative error of at most 0.00035.
Values may be sent and summed in bfloat16 or wider, within the bound.
A program may use at most 128 MiB of HBM per device.

v0:
```python
import math

import jax
import jax.numpy as jnp
from jax import lax
from jax.sharding import PartitionSpec as P

HEAD_WIDTH = 128
N = 128
HQ_DEV = 8
KV_DEV = 1


very_negative = -1e30
highest = lax.Precision.HIGHEST


def prefix(value, axis, join, neutral):
    count, mine = (lax.axis_size(axis), lax.axis_index(axis))
    pieces = jax.tree.map(lambda part: lax.all_gather(part, axis), value)
    subtotal = jax.tree.map(
        lambda part, zero: jnp.full_like(part, 0) + jnp.asarray(zero, part.dtype), value, neutral
    )

    def hop(position, subtotal):
        longer = join(subtotal, jax.tree.map(lambda part: part[position], pieces))
        return jax.tree.map(lambda new, old: jnp.where(position < mine, new, old), longer, subtotal)

    return lax.fori_loop(0, count - 1, hop, subtotal)


def chain_step(earlier, later):
    return (earlier[0] + later[0], jnp.exp(later[0])[:, None, None] * earlier[1] + later[1])


def attend_rows(current, query_head_rows, query_pos, key_piece, value_piece):
    row_top, denominator, mixture = current
    piece_rows = key_piece.shape[0]
    kv_heads = query_head_rows.shape[1]
    key_head_rows = key_piece.reshape(piece_rows, kv_heads, HEAD_WIDTH)
    value_head_rows = value_piece.reshape(piece_rows, kv_heads, HEAD_WIDTH)
    scores = jnp.einsum(
        "qkgd,nkd->qkgn", query_head_rows, key_head_rows, precision=highest
    ) / math.sqrt(HEAD_WIDTH)
    key_pos = jnp.arange(piece_rows, dtype=jnp.int32)
    allowed = (key_pos[None, :] <= query_pos[:, None])[:, None, None, :]
    scores = jnp.where(allowed, scores, very_negative)
    new_top = jnp.maximum(row_top, jnp.max(scores, axis=-1))
    weights = jnp.where(allowed, jnp.exp(scores - new_top[..., None]), 0.0)
    denominator = jnp.sum(weights, axis=-1)
    mixture = jnp.einsum("qkgn,nkd->qkgd", weights, value_head_rows, precision=highest)
    return (new_top, denominator, mixture)


def local(queries, keys, values, inputs_x, in_b, in_c, log_decay):
    row_count = queries.shape[0]
    group_width = HQ_DEV // KV_DEV
    seq_count = lax.axis_size("seq")
    own_index = lax.axis_index("seq")
    first_query = own_index * row_count
    query_sets = ((queries, first_query + jnp.arange(row_count, dtype=jnp.int32)),)
    head_sets = tuple(
        (
            rows.astype(jnp.float32).reshape(rows.shape[0], KV_DEV, group_width, HEAD_WIDTH)
            for rows, positions in query_sets
        )
    )
    pos_sets = tuple((positions for rows, positions in query_sets))
    start_state = tuple(
        (
            (
                jnp.full((positions.shape[0], KV_DEV, group_width), very_negative, jnp.float32),
                jnp.zeros((positions.shape[0], KV_DEV, group_width), jnp.float32),
                jnp.zeros((positions.shape[0], KV_DEV, group_width, HEAD_WIDTH), jnp.float32),
            )
            for positions in pos_sets
        )
    )
    key_piece = lax.all_gather(keys.astype(jnp.float32), "seq", axis=0, tiled=True)
    value_piece = lax.all_gather(values, "seq", axis=0, tiled=True)
    updated = []
    for current, query_head_rows, query_pos in zip(start_state, head_sets, pos_sets):

        def compute(state_now, query_head_rows=query_head_rows, query_pos=query_pos):
            return attend_rows(state_now, query_head_rows, query_pos, key_piece, value_piece)

        updated.append(compute(current))
    finished = tuple(updated)
    outputs = [
        (mixture / denominator[..., None]).reshape(mixture.shape[0], HQ_DEV, HEAD_WIDTH)
        for row_top, denominator, mixture in finished
    ]
    teacher_out = outputs[0]
    c_scale = 0.5 / math.sqrt(N * row_count * seq_count)
    student_x = inputs_x.astype(jnp.float32).reshape(row_count, HQ_DEV, HEAD_WIDTH)
    b_rows = in_b.astype(jnp.float32)
    c_rows = in_c.astype(jnp.float32) * c_scale
    cumulative = jnp.cumsum(log_decay, axis=0)
    totals = cumulative[-1]
    heads_first = cumulative.T
    causal = jnp.arange(row_count)[:, None] >= jnp.arange(row_count)[None, :]
    decays = jnp.exp(
        jnp.where(causal[None], heads_first[:, :, None] - heads_first[:, None, :], -jnp.inf)
    )
    inner_products = jnp.dot(in_c, in_b.T, preferred_element_type=jnp.float32) * c_scale
    mixing = decays * inner_products[None]
    rising = jnp.exp(cumulative)
    ending = jnp.exp(totals[None, :] - cumulative)
    local_state = jnp.einsum(
        "shp,sn->hpn", student_x * ending[:, :, None], b_rows, precision=highest
    )
    identity = (jnp.zeros_like(totals), jnp.zeros_like(local_state))
    prefix_log, state_in = prefix((totals, local_state), "seq", chain_step, identity)
    y_intra = jnp.einsum("hts,shp->thp", mixing, student_x, precision=highest)
    y_inter = jnp.einsum("tn,hpn->thp", c_rows, state_in, precision=highest) * rising[:, :, None]
    mismatch = y_intra + y_inter - teacher_out
    scaled_mismatch = mismatch * rising[:, :, None]
    local_grad = jnp.einsum("thp,tn->hpn", scaled_mismatch, c_rows, precision=highest)
    grad_pieces = lax.all_gather(local_grad[None], "seq", axis=0, tiled=True)
    log_pieces = lax.all_gather(prefix_log[None], "seq", axis=0, tiled=True)
    shard_ids = jnp.arange(grad_pieces.shape[0], dtype=jnp.int32)
    log_gaps = jnp.where(
        (shard_ids > own_index)[:, None], log_pieces - (prefix_log + totals)[None, :], -jnp.inf
    )
    later_grad = jnp.zeros_like(local_grad) + jnp.einsum(
        "ch,chpn->hpn", jnp.exp(log_gaps), grad_pieces, precision=highest
    )
    grad_x = jnp.einsum("hts,thp->shp", mixing, mismatch, precision=highest)
    grad_x = (
        grad_x
        + jnp.einsum("hpn,sn->shp", later_grad, b_rows, precision=highest) * ending[:, :, None]
    )
    products = jnp.einsum("thp,shp->hts", mismatch, student_x, precision=highest)
    weighted = decays * products
    grad_b = jnp.einsum("hts,tn->sn", weighted, c_rows, precision=highest)
    grad_b = grad_b + jnp.einsum(
        "shp,hpn->sn", student_x * ending[:, :, None], later_grad, precision=highest
    )
    grad_c = jnp.einsum("hts,sn->tn", weighted, b_rows, precision=highest)
    grad_c = grad_c + jnp.einsum("thp,hpn->tn", scaled_mismatch, state_in, precision=highest)
    summed_b, summed_c = (
        lax.psum_scatter(grad_b, "mp", scatter_dimension=0, tiled=True),
        lax.psum_scatter(grad_c, "mp", scatter_dimension=0, tiled=True),
    )
    return (grad_x.reshape(row_count, HQ_DEV * HEAD_WIDTH), summed_b, summed_c * c_scale)


def solution(mesh):
    in_specs = (
        P("seq", "mp"),
        P("seq", "mp"),
        P("seq", "mp"),
        P("seq", "mp"),
        P("seq", None),
        P("seq", None),
        P("seq", "mp"),
    )
    out_specs = (P("seq", "mp"), P(("seq", "mp"), None), P(("seq", "mp"), None))
    return jax.shard_map(local, mesh=mesh, in_specs=in_specs, out_specs=out_specs, check_vma=False)
```

profile of v0, /device:TPU:0, one launch (start us, length us, event | category | flops | bytes accessed | tf_op | source)
XLA Modules:
  0.0 302.7 jit_solution(4650409875436568659)
XLA Ops:
  7.2 1.4 convert_element_type.10
  11.7 1.9 fusion.33
  13.8 23.0 %all-gather.3 = f32[16,1,8]{2,1,0:T(1,128)S(1)} all-gather(f32[1,1,8]{2,1,0:T(1,128)S(1)} %get-tuple-element.180), channel_id=1, replica_groups=mesh['seq'=16,'mp'=2] {'seq'}, dimensions={0}, use_global_device_ids=true | all-gather | bytes 544 | tf_op jit(solution)/shard_map/all_gather | solution.py:20
  38.6 12.3 %all-gather.9.cloned.1.call-done = f32[2048,128]{1,0:T(8,128)} async-done(((f32[128,128]{1,0:T(8,128)}), f32[2048,128]{1,0:T(8,128)}) %all-gather.9.cloned.1.call-update) | async-done | bytes 1048592 | tf_op jit(solution)/shard_map/all_gather | solution.py:79
  50.9 5.5 %fusion.5 = (f32[128,8]{0,1:T(8,128)S(1)}, f32[2048,128,8]{1,0,2:T(8,128)S(1)}) fusion(pred[128,2048]{0,1:T(8,128)(4,1)S(1)} %iota_compare_fusion, f32[2048,128]{1,0:T(8,128)} %all-gather.9.cloned.1.call-done, bf16[128,1024]{1,0:T(8,128)(2,1)S(1)} %copy-done), kind=kOutput, calls=%fused_computation.12 | convolution fusion | flops 3227515904 | bytes 9965568 | tf_op jit(solution)/shard_map/qkgd,nkd->qkgn/dot_general | solution.py:42
  56.4 3.2 %copy-done.1 = f32[2048,128,8]{1,0,2:T(8,128)} copy-done((f32[2048,128,8]{1,0,2:T(8,128)}, f32[2048,128,8]{1,0,2:T(8,128)S(1)}, u32[]{:S(2)}) %copy-start.1) | copy-done | bytes 8388632
  59.6 2.0 fusion.6
  61.6 28.3 %all-gather.11.cloned.1.call-done = f32[2048,128]{1,0:T(8,128)} async-done(((f32[128,128]{1,0:T(8,128)}), f32[2048,128]{1,0:T(8,128)}) %all-gather.11.cloned.1.call-update) | async-done | bytes 1048592 | tf_op jit(solution)/shard_map/all_gather | solution.py:80
  89.9 16.9 %fusion.28 = f32[128,8,128]{2,0,1:T(8,128)S(1)} fusion(f32[2048,128]{1,0:T(8,128)} %all-gather.11.cloned.1.call-done, f32[2048,128,8]{1,0,2:T(8,128)} %copy-done.1, f32[128,8]{0,1:T(8,128)S(1)} %broadcast_maximum_fusion, pred[128,2048]{0,1:T(8,128)(4,1)S(1)} %iota_compare_fusion, f32[128,8]{0,1:T(8,128)S(1)} %fusion.6), kind=kOutput, calls=%fused_computation.40 | convolution fusion | flops 3229745152 | bytes 10231808 | tf_op jit(solution)/shard_map/qkgn,nkd->qkgd/dot_general | solution.py:51
  106.8 59.7 %all-gather.13.cloned.1.call-done = f32[128,128,128]{2,1,0:T(8,128)} async-done(((f32[8,128,128]{2,1,0:T(8,128)}), f32[128,128,128]{2,1,0:T(8,128)}) %all-gather.13.cloned.1.call-update) | async-done | bytes 8388624 | tf_op jit(solution)/shard_map/all_gather | solution.py:20
  166.5 18.3 %while.16 = (s32[]{:T(128)}, f32[8]{0:T(128)S(1)}, f32[8,128,128]{2,1,0:T(8,128)S(1)}, s32[]{:T(128)}, f32[16,8]{1,0:T(8,128)S(1)}, /*index=5*/f32[16,8,128,128]{3,2,1,0:T(8,128)}, s32[]{:T(128)}, s32[]{:T(128)}) while((s32[]{:T(128)}, f32[8]{0:T(128)S(1)}, f32[8,128,128]{2,1,0:T(8,128)S(1)}, s32[]{:T(128)}, ...), condition=%wide.region_2.3_spmd.clone, body=%wide.region_1.2_spmd.clone.sunk | while | flops 524316 | bytes 1573139 | solution.py:29
  167.7 1.2 fusion.89
  169.0 1.2 fusion.89
  180.0 1.2 fusion.89
  181.2 1.2 fusion.89
  182.4 1.2 fusion.89
  183.6 1.2 fusion.89
  187.4 1.9 fusion.38
  191.0 31.5 %all-reduce = f32[128]{0:T(128)S(1)} all-reduce(f32[128]{0:T(128)S(1)} %dynamic-update-slice), channel_id=3, replica_groups=mesh['seq'=16,'mp'=2] {'seq'}, use_global_device_ids=true, to_apply=%add | all-reduce | flops 128 | bytes 1024
  222.7 1.2 convolution_bitcast_fusion.2
  223.9 1.4 broadcast_multiply_fusion
  225.3 48.0 %all-gather.15.cloned.1.call-done = f32[128,128,128]{2,1,0:T(8,128)} async-done(((f32[8,128,128]{2,1,0:T(8,128)}), f32[128,128,128]{2,1,0:T(8,128)}) %all-gather.15.cloned.1.call-update) | async-done | bytes 8388624 | tf_op jit(solution)/shard_map/all_gather | solution.py:119
  273.3 12.3 %fusion.3 = f32[8,1,128,128]{3,1,2,0:T(1,128)S(1)} fusion(f32[16,8,1,1]{0,2,3,1:T(1,128)S(1)} %copy.62, f32[16,8,128,128]{3,2,1,0:T(8,128)} %bitcast.127), kind=kOutput, calls=%fused_computation.9 | convolution fusion | flops 25165824 | bytes 8913408 | tf_op jit(solution)/shard_map/ch,chpn->hpn/dot_general | solution.py:125
  289.0 6.9 %reduce-scatter.3.cloned.1.call-done = f32[64,128]{1,0:T(8,128)} async-done(((f32[128,128]{1,0:T(8,128)}), f32[64,128]{1,0:T(8,128)}) %reduce-scatter.3.cloned.1.call-update) | async-done | bytes 32784 | tf_op jit(solution)/shard_map/reduce_scatter | solution.py:142
  (78 shorter events, 22.9 us)
Async XLA Ops:
  7.2 43.7 %copy-start = (bf16[128,1024]{1,0:T(8,128)(2,1)S(1)}, bf16[128,1024]{1,0:T(8,128)(2,1)}, u32[]{:S(2)}) copy-start(bf16[128,1024]{1,0:T(8,128)(2,1)} %param.9) | copy-start | bytes 786436
  7.2 43.7 %all-gather.9.cloned.1.call-start = ((), (), s32[]{:S(2)}) async-start(), calls=%async_computation.2 | async-start | bytes 1114112 | tf_op jit(solution)/shard_map/all_gather | solution.py:79
  8.7 81.3 %all-gather.11.cloned.1.call-start = ((), (), s32[]{:S(2)}) async-start(), calls=%async_computation.3 | async-start | bytes 1114112 | tf_op jit(solution)/shard_map/all_gather | solution.py:80
  9.4 157.1 %all-gather.13.cloned.1.call-start = ((), (), s32[]{:S(2)}) async-start(), calls=%async_computation.6 | async-start | bytes 8912896 | tf_op jit(solution)/shard_map/all_gather | solution.py:20
  13.6 210.3 %reduce-scatter.5.cloned.1.call-start = ((), (), s32[]{:S(2)}) async-start(), calls=%async_computation.5 | async-start | bytes 98304 | tf_op jit(solution)/shard_map/reduce_scatter | solution.py:143
  56.3 3.2 %copy-start.1 = (f32[2048,128,8]{1,0,2:T(8,128)}, f32[2048,128,8]{1,0,2:T(8,128)S(1)}, u32[]{:S(2)}) copy-start(f32[2048,128,8]{1,0,2:T(8,128)S(1)} %get-tuple-element.182) | copy-start | bytes 25165828
  61.6 123.2 %copy-start.2 = (bf16[128,128]{1,0:T(8,128)(2,1)S(1)}, bf16[128,128]{1,0:T(8,128)(2,1)}, u32[]{:S(2)}) copy-start(bf16[128,128]{1,0:T(8,128)(2,1)} %param.14) | copy-start | bytes 98308
  106.8 79.8 %copy-start.3 = (bf16[128,128]{1,0:T(8,128)(2,1)S(1)}, bf16[128,128]{1,0:T(8,128)(2,1)}, u32[]{:S(2)}) copy-start(bf16[128,128]{1,0:T(8,128)(2,1)} %param.13) | copy-start | bytes 98308
  106.8 82.7 %copy-start.4 = (u32[32]{0:T(128)S(1)}, u32[32]{0:T(128)}, u32[]{:S(2)}) copy-start(u32[32]{0:T(128)} %constant.52) | copy-start | bytes 388
  187.4 85.9 %all-gather.15.cloned.1.call-start = ((), (), s32[]{:S(2)}) async-start(), calls=%async_computation.7 | async-start | bytes 8912896 | tf_op jit(solution)/shard_map/all_gather | solution.py:119
  189.4 106.5 %reduce-scatter.3.cloned.1.call-start = ((), (), s32[]{:S(2)}) async-start(), calls=%async_computation.4 | async-start | bytes 98304 | tf_op jit(solution)/shard_map/reduce_scatter | solution.py:142
Sparse Core Ops, SparseCore 0:
  10.2 40.6 all-gather.8
  53.0 36.8 all-gather.10
  92.7 73.7 all-gather.12
  187.5 8.1 reduce-scatter.4
  198.3 75.0 all-gather.14
  287.7 8.1 reduce-scatter.2
where the time goes:
time: 304 us; the launch traced here: 303 us
  waiting for transfers between devices  156 us (51%)
  blocking collectives  54.4 us (18%)
  matrix products  46.2 us (15%)
  other arithmetic  23.2 us (8%)
  between operations  15 us (5%)
  local copies, waits for them, and re-layouts  7.31 us (2%)
    all_gather x1, waiting for transfers between devices, prefix(): pieces = jax.tree.map(lambda part: lax.all_gather(part, axis), value)  59.7 us
    all_gather x1, waiting for transfers between devices, local(): grad_pieces = lax.all_gather(local_grad[None], 'seq', axis=0, tiled=True)  48 us
    unnamed x1, blocking collectives  31.5 us
    all_gather x1, waiting for transfers between devices, local(): value_piece = lax.all_gather(values, 'seq', axis=0, tiled=True)  28.3 us
    all_gather x1, blocking collectives, prefix(): pieces = jax.tree.map(lambda part: lax.all_gather(part, axis), value)  23 us
    select_n x15, other arithmetic, hop(): jnp.where(position < mine, new, old)  17.6 us
    dot_general x1, matrix products, attend_rows(): jnp.einsum('qkgn,nkd->qkgd', weights, value_head_rows, precision=highest)  16.9 us
    dot_general x1, matrix products, local(): jnp.einsum('ch,chpn->hpn', jnp.exp(log_gaps), grad_pieces, precision=high...  12.3 us
  transfers between devices with their start and end apart: 6, of which 5 were waited for; matrix products, arithmetic and copies ran while one was open for 12% of the time, Pallas kernels for 0%

commit v1 on v0

v1 whole, which is shorter than its diff:
```python
import functools
import math

import jax
import jax.numpy as jnp
from jax import lax
from jax.experimental import pallas as pl
from jax.experimental.pallas import tpu as pltpu
from jax.sharding import PartitionSpec as P

W = 128
HEADS = 8
PLANE = 4
MESH = pl.DeviceIdType.MESH
F32 = jnp.float32
BF = jnp.bfloat16
LOW = -1e30


def dot(a, b):
    return lax.dot_general(a, b, (((1,), (0,)), ((), ())), preferred_element_type=F32)


def dot_nt(a, b):
    return lax.dot_general(a, b, (((1,), (1,)), ((), ())), preferred_element_type=F32)


def split(v):
    hi = v.astype(BF)
    return hi, (v - hi.astype(F32)).astype(BF)


def kernel(
    planes, mp, c_scale,
    q_ref, k_ref, v_ref, x_ref, b_ref, c_ref, ld_ref,
    gx_ref, gb_ref, gc_ref,
    kv, cum, lsend, rs, zin, zout, ag_out, s_in,
    lgsend, rsb, zinb, zoutb, agb_out, g_in,
    decay, mixt, ybuf, acc, top, den, qs, dbuf, gsum, mpb,
    kv_r, col_s, x_s, core_s, diag_s,
    rs_s, rs_r, z_s, z_r, ag_s, ag_r,
    rsb_s, rsb_r, zb_s, zb_r, agb_s, agb_r,
    mp_s, mp_r,
):
    s = lax.axis_index("seq")
    m = lax.axis_index("mp")
    z = s // PLANE
    r = s % PLANE
    base = z * PLANE
    core = r % 2
    rx = (r + 2) % PLANE
    rc = r + 1 - 2 * core
    rd = (rc + 2) % PLANE
    up = lax.rem(s + PLANE, planes * PLANE)
    down = lax.rem(s + (planes - 1) * PLANE, planes * PLANE)
    not_last = z < planes - 1
    not_first = z > 0
    rows = W // mp

    barrier = pltpu.get_barrier_semaphore()
    for k in range(1, PLANE):
        pl.semaphore_signal(
            barrier, inc=1, device_id=(base + (r + k) % PLANE, m), device_id_type=MESH
        )
    for k in range(1, mp):
        pl.semaphore_signal(barrier, inc=1, device_id=(s, (m + k) % mp), device_id_type=MESH)

    @pl.when(not_last)
    def _():
        pl.semaphore_signal(barrier, inc=1, device_id=(up, m), device_id_type=MESH)

    @pl.when(not_first)
    def _():
        pl.semaphore_signal(barrier, inc=1, device_id=(down, m), device_id_type=MESH)

    v_hi, v_lo = split(v_ref[...])
    kv[z, r, :, 0:W] = k_ref[...]
    kv[z, r, :, W : 2 * W] = v_hi
    kv[z, r, :, 2 * W : 3 * W] = v_lo

    extra = jnp.where(not_last, 1, 0) + jnp.where(not_first, 1, 0)
    pl.semaphore_wait(barrier, PLANE - 1 + mp - 1 + extra)

    def remote(src, dst, send, recv, to):
        return pltpu.make_async_remote_copy(
            src_ref=src, dst_ref=dst, send_sem=send, recv_sem=recv,
            device_id=to, device_id_type=MESH,
        )

    def kv_copy(zp, rr, send, to):
        return remote(kv.at[zp, rr], kv.at[zp, rr], send.at[zp], kv_r.at[zp, rr], to)

    def col(zp):
        return kv_copy(zp, r, col_s, (up, m))

    def across(zp):
        return kv_copy(zp, r, x_s, (base + rx, m))

    def chip(zp):
        return kv_copy(zp, r, core_s, (base + rc, m))

    def diag(zp):
        return kv_copy(zp, rx, diag_s, (base + rc, m))

    def arrived(zp, rr):
        kv_copy(zp, rr, col_s, (base + rc, m)).wait_recv()

    def spread(zp):
        @pl.when(not_last)
        def _():
            col(zp).start()

        across(zp).start()
        chip(zp).start()

    spread(z)

    at_row = lax.broadcasted_iota(jnp.int32, (W, W), 0)
    at_col = lax.broadcasted_iota(jnp.int32, (W, W), 1)
    tri = jnp.where(at_row >= at_col, 1.0, 0.0).astype(BF)
    ld = ld_ref[...]
    for h in range(HEADS):
        wide = jnp.broadcast_to(ld[:, h : h + 1], (W, W))
        p0 = wide.astype(BF)
        rest = wide - p0.astype(F32)
        p1 = rest.astype(BF)
        p2 = (rest - p1.astype(F32)).astype(BF)
        cum[h] = dot(tri, p0) + dot(tri, p1) + dot(tri, p2)

    b = b_ref[...]
    c = c_ref[...]
    b_t = b.astype(F32).T.astype(BF)
    c_t = c.astype(F32).T.astype(BF)

    def head(ref, h):
        return ref[:, h * W : (h + 1) * W]

    for o in range(PLANE):
        for g in range(2):
            h = 2 * o + g
            total = cum[h, W - 1 : W, :]
            ending = jnp.exp(total - cum[h])
            hi, lo = split(head(x_ref, h).astype(F32) * ending)
            lsend[o, g, 0:W, :] = dot(b_t, hi) + dot(b_t, lo)
            lsend[o, g, W : W + 8, :] = jnp.broadcast_to(total, (8, W))

    def rs_copy(k):
        o = (r + k) % PLANE
        return remote(lsend.at[o], rs.at[r], rs_s.at[k], rs_r.at[r], (base + o, m))

    def rs_arrive(k):
        o = (r + k) % PLANE
        return remote(lsend.at[o], rs.at[o], rs_s.at[k], rs_r.at[o], (base + o, m))

    for k in range(1, PLANE):
        rs_copy(k).start()
    rs[r] = lsend[r]

    cb = dot_nt(c, b) * c_scale
    cb_t = dot_nt(b, c) * c_scale
    for h in range(HEADS):
        here = cum[h]
        other = here.T
        dec = jnp.exp(jnp.where(at_row >= at_col, here - other, LOW))
        dec_t = jnp.exp(jnp.where(at_row <= at_col, other - here, LOW))
        decay[h] = dec
        hi, lo = split(dec_t * cb_t)
        mixt[0, h] = hi
        mixt[1, h] = lo
        hi, lo = split(dec * cb)
        xh = head(x_ref, h)
        ybuf[h] = dot(hi, xh) + dot(lo, xh)
        qs[h] = head(q_ref, h)

    def forward_piece(i, carry):
        zp = z - 1 - i
        arrived(zp, r)
        spread(zp)
        return carry

    lax.fori_loop(0, z, forward_piece, 0)

    def plane_ready(zp):
        arrived(zp, rx)
        diag(zp).start()
        arrived(zp, rc)
        arrived(zp, rd)

    factor = math.log2(math.e) / math.sqrt(W)

    def attend(zp, first):
        keys = kv[zp, :, :, 0:W].reshape(PLANE * W, W)
        both = kv[zp, :, :, W : 3 * W].reshape(PLANE * W, 2 * W)
        v_top = kv[zp, :, :, W : 2 * W].reshape(PLANE * W, W)
        for h in range(HEADS):
            sc = dot_nt(qs[h], keys) * factor
            if first:
                t = lax.broadcasted_iota(jnp.int32, (W, PLANE * W), 0) + r * W
                u = lax.broadcasted_iota(jnp.int32, (W, PLANE * W), 1)
                sc = jnp.where(u <= t, sc, LOW)
            new = jnp.max(sc, axis=-1, keepdims=True)
            if not first:
                old = top[h][:, 0:1]
                new = jnp.maximum(old, new)
                scale = jnp.exp2(old - new)
            wt = jnp.exp2(sc - new)
            total = jnp.sum(wt, axis=-1, keepdims=True)
            hi, lo = split(wt)
            res = dot(hi, both)
            mix = res[:, 0:W] + res[:, W:] + dot(lo, v_top)
            if first:
                acc[h] = mix
                den[h] = jnp.broadcast_to(total, (W, W))
            else:
                acc[h] = acc[h] * scale + mix
                den[h] = den[h] * scale + total
            top[h] = jnp.broadcast_to(new, (W, W))

    plane_ready(z)
    attend(z, True)

    def attend_earlier(i, carry):
        zp = z - 1 - i
        plane_ready(zp)
        attend(zp, False)
        return carry

    def z_copy(g):
        return remote(zout.at[g], zin.at[g], z_s.at[g], z_r.at[g], (up, m))

    def ag_copy(k, g):
        o = (r + k) % PLANE
        return remote(
            ag_out.at[o, g], s_in.at[r, g], ag_s.at[k, g], ag_r.at[r, g], (base + o, m)
        )

    def ag_arrive(k, g):
        o = (r + k) % PLANE
        return remote(
            ag_out.at[o, g], s_in.at[o, g], ag_s.at[k, g], ag_r.at[o, g], (base + o, m)
        )

    before = jnp.where(not_last, 0, z)
    lax.fori_loop(0, before, attend_earlier, 0)

    for k in range(1, PLANE):
        rs_arrive(k).wait_recv()

    for g in range(2):
        pres, coefs = [None], [None]
        pre, coef = None, None
        for j in range(PLANE):
            e = jnp.exp(rs[j, g, W : W + 1, :])
            local = rs[j, g, 0:W, :]
            pre = local if pre is None else e * pre + local
            coef = e if coef is None else coef * e
            pres.append(pre)
            coefs.append(coef)

        @pl.when(not_first)
        def _():
            z_copy(g).wait_recv()

        @pl.when(jnp.logical_not(not_first))
        def _():
            zin[g] = jnp.zeros((W, W), F32)

        came = zin[g]
        zout[g] = coefs[PLANE] * came + pres[PLANE]

        @pl.when(not_last)
        def _():
            z_copy(g).start()

        for j in range(PLANE):
            ag_out[j, g] = came if j == 0 else coefs[j] * came + pres[j]
        for k in range(1, PLANE):
            ag_copy(k, g).start()
        s_in[r, g] = ag_out[r, g]

    lax.fori_loop(before, z, attend_earlier, 0)

    for k in range(1, PLANE):
        for g in range(2):
            ag_arrive(k, g).wait_recv()

    for o in range(PLANE):
        for g in range(2):
            h = 2 * o + g
            rising = jnp.exp(cum[h])
            hi, lo = split(s_in[o, g])
            inter = (dot(c, hi) + dot(c, lo)) * (rising * c_scale)
            d = ybuf[h] + inter - acc[h] / den[h]
            dbuf[h] = d
            hi, lo = split(d * rising)
            lgsend[o, g] = (dot(c_t, hi) + dot(c_t, lo)) * c_scale

    def rsb_copy(k):
        o = (r + k) % PLANE
        return remote(lgsend.at[o], rsb.at[r], rsb_s.at[k], rsb_r.at[r], (base + o, m))

    def rsb_arrive(k):
        o = (r + k) % PLANE
        return remote(lgsend.at[o], rsb.at[o], rsb_s.at[k], rsb_r.at[o], (base + o, m))

    for k in range(1, PLANE):
        rsb_copy(k).start()
    rsb[r] = lgsend[r]

    weighted = jnp.zeros((W, W), F32)
    grad_c = jnp.zeros((W, W), F32)
    for h in range(HEADS):
        d_hi, d_lo = split(dbuf[h])
        xh = head(x_ref, h)
        weighted += decay[h] * (dot_nt(d_hi, xh) + dot_nt(d_lo, xh))
        s_hi, s_lo = split(s_in[h // 2, h % 2])
        inter = dot_nt(d_hi, s_hi) + dot_nt(d_hi, s_lo) + dot_nt(d_lo, s_hi)
        grad_c += jnp.exp(cum[h]) * inter
        gx_ref[:, h * W : (h + 1) * W] = (
            dot(mixt[0, h], d_hi) + dot(mixt[0, h], d_lo) + dot(mixt[1, h], d_hi)
        )
    hi, lo = split(weighted)
    grad_c = (grad_c + dot(hi, b) + dot(lo, b)) * c_scale
    hi, lo = split(weighted.T)
    gsum[0] = (dot(hi, c) + dot(lo, c)) * c_scale
    gsum[1] = grad_c

    def mp_copy(k, which):
        to = (m + k) % mp
        return remote(
            gsum.at[which, pl.ds(pl.multiple_of(to * rows, 8), rows)],
            mpb.at[k - 1, which],
            mp_s.at[k - 1, which], mp_r.at[k - 1, which], (s, to),
        )

    for k in range(1, mp):
        mp_copy(k, 1).start()

    def zb_copy(g):
        return remote(zoutb.at[g], zinb.at[g], zb_s.at[g], zb_r.at[g], (down, m))

    def agb_copy(k, g):
        o = (r + k) % PLANE
        return remote(
            agb_out.at[o, g], g_in.at[r, g], agb_s.at[k, g], agb_r.at[r, g], (base + o, m)
        )

    def agb_arrive(k, g):
        o = (r + k) % PLANE
        return remote(
            agb_out.at[o, g], g_in.at[o, g], agb_s.at[k, g], agb_r.at[o, g], (base + o, m)
        )

    for k in range(1, PLANE):
        rsb_arrive(k).wait_recv()

    for g in range(2):
        sufs, coefs = {PLANE - 1: None}, {PLANE - 1: None}
        suf, coef = None, None
        for j in range(PLANE - 1, -1, -1):
            e = jnp.exp(rs[j, g, W : W + 1, :])
            local = rsb[j, g]
            suf = local if suf is None else e * suf + local
            coef = e if coef is None else coef * e
            sufs[j - 1] = suf
            coefs[j - 1] = coef

        @pl.when(not_last)
        def _():
            zb_copy(g).wait_recv()

        @pl.when(jnp.logical_not(not_last))
        def _():
            zinb[g] = jnp.zeros((W, W), F32)

        came = zinb[g]
        zoutb[g] = coefs[-1] * came + sufs[-1]

        @pl.when(not_first)
        def _():
            zb_copy(g).start()

        for j in range(PLANE):
            agb_out[j, g] = came if j == PLANE - 1 else coefs[j] * came + sufs[j]
        for k in range(1, PLANE):
            agb_copy(k, g).start()
        g_in[r, g] = agb_out[r, g]

    for k in range(1, PLANE):
        for g in range(2):
            agb_arrive(k, g).wait_recv()

    grad_b = gsum[0]
    for o in range(PLANE):
        for g in range(2):
            h = 2 * o + g
            ending = jnp.exp(cum[h, W - 1 : W, :] - cum[h])
            hi, lo = split(g_in[o, g])
            gx_ref[:, h * W : (h + 1) * W] += (dot(b, hi) + dot(b, lo)) * ending
            xh = head(x_ref, h)
            grad_b += (dot_nt(xh, hi) + dot_nt(xh, lo)) * ending
    gsum[0] = grad_b
    for k in range(1, mp):
        mp_copy(k, 0).start()

    for k in range(1, PLANE):
        rs_copy(k).wait_send()
        rsb_copy(k).wait_send()
        for g in range(2):
            ag_copy(k, g).wait_send()
            agb_copy(k, g).wait_send()

    def sent(zp, carry):
        @pl.when(not_last)
        def _():
            col(zp).wait_send()

        across(zp).wait_send()
        chip(zp).wait_send()
        diag(zp).wait_send()
        return carry

    lax.fori_loop(0, z + 1, sent, 0)

    @pl.when(not_last)
    def _():
        for g in range(2):
            z_copy(g).wait_send()

    @pl.when(not_first)
    def _():
        for g in range(2):
            zb_copy(g).wait_send()

    own = pl.ds(pl.multiple_of(m * rows, 8), rows)
    for which, out in ((1, gc_ref), (0, gb_ref)):
        total = gsum[which, own]
        for k in range(1, mp):
            mp_copy(k, which).wait_recv()
            total += mpb[k - 1, which]
        out[...] = total
    for which in range(2):
        for k in range(1, mp):
            mp_copy(k, which).wait_send()


def local(queries, keys, values, inputs_x, in_b, in_c, log_decay):
    tokens = queries.shape[0]
    seq = lax.axis_size("seq")
    mp = lax.axis_size("mp")
    planes = seq // PLANE
    c_scale = 0.5 / math.sqrt(W * tokens * seq)
    dma = pltpu.SemaphoreType.DMA
    scratch = [
        pltpu.VMEM((planes, PLANE, W, 3 * W), BF),
        pltpu.VMEM((HEADS, W, W), F32),
        pltpu.VMEM((PLANE, 2, W + 8, W), F32),
        pltpu.VMEM((PLANE, 2, W + 8, W), F32),
        pltpu.VMEM((2, W, W), F32),
        pltpu.VMEM((2, W, W), F32),
        pltpu.VMEM((PLANE, 2, W, W), F32),
        pltpu.VMEM((PLANE, 2, W, W), F32),
        pltpu.VMEM((PLANE, 2, W, W), F32),
        pltpu.VMEM((PLANE, 2, W, W), F32),
        pltpu.VMEM((2, W, W), F32),
        pltpu.VMEM((2, W, W), F32),
        pltpu.VMEM((PLANE, 2, W, W), F32),
        pltpu.VMEM((PLANE, 2, W, W), F32),
        pltpu.VMEM((HEADS, W, W), F32),
        pltpu.VMEM((2, HEADS, W, W), BF),
        pltpu.VMEM((HEADS, W, W), F32),
        pltpu.VMEM((HEADS, W, W), F32),
        pltpu.VMEM((HEADS, W, W), F32),
        pltpu.VMEM((HEADS, W, W), F32),
        pltpu.VMEM((HEADS, W, W), BF),
        pltpu.VMEM((HEADS, W, W), F32),
        pltpu.VMEM((2, W, W), F32),
        pltpu.VMEM((max(mp - 1, 1), 2, W // mp, W), F32),
        dma((planes, PLANE)), dma((planes,)), dma((planes,)), dma((planes,)), dma((planes,)),
        dma((PLANE,)), dma((PLANE,)), dma((2,)), dma((2,)), dma((PLANE, 2)), dma((PLANE, 2)),
        dma((PLANE,)), dma((PLANE,)), dma((2,)), dma((2,)), dma((PLANE, 2)), dma((PLANE, 2)),
        dma((max(mp - 1, 1), 2)), dma((max(mp - 1, 1), 2)),
    ]
    vmem = pl.BlockSpec(memory_space=pltpu.VMEM)
    return pl.pallas_call(
        functools.partial(kernel, planes, mp, c_scale),
        out_shape=(
            jax.ShapeDtypeStruct((tokens, HEADS * W), F32),
            jax.ShapeDtypeStruct((tokens // mp, W), F32),
            jax.ShapeDtypeStruct((tokens // mp, W), F32),
        ),
        in_specs=[vmem] * 7,
        out_specs=(vmem,) * 3,
        scratch_shapes=scratch,
        compiler_params=pltpu.CompilerParams(
            collective_id=0, has_side_effects=True, vmem_limit_bytes=40 << 20
        ),
        cost_estimate=pl.CostEstimate(
            flops=4_000_000_000, bytes_accessed=2_000_000, transcendentals=2_500_000
        ),
    )(queries, keys, values, inputs_x, in_b, in_c, log_decay)


def solution(mesh):
    in_specs = (
        P("seq", "mp"), P("seq", "mp"), P("seq", "mp"), P("seq", "mp"),
        P("seq", None), P("seq", None), P("seq", "mp"),
    )
    out_specs = (P("seq", "mp"), P(("seq", "mp"), None), P(("seq", "mp"), None))
    return jax.shard_map(local, mesh=mesh, in_specs=in_specs, out_specs=out_specs, check_vma=False)
```

time: 304 us -> 73.1 us (0.24)
  waiting for transfers between devices: 156 us -> 0 us
  Pallas kernels: 0 us -> 64.9 us
  blocking collectives: 54.4 us -> 0 us
  matrix products: 46.2 us -> 0 us
  other arithmetic: 23.2 us -> 0 us
  between operations: 15 us -> 0.66 us
    all_gather x4 -> x0, waiting for transfers between devices: 148 us -> none  [the longest x1 59.7 us: prefix(): pieces = jax.tree.map(lambda part: lax.all_gather(part, axis), value)]
    pallas_call x0 -> x1, Pallas kernels: none -> 64.9 us  [local(): pl.pallas_call(functools.partial(kernel, planes, mp, c_scale), out_shape=...]
    dot_general x15 -> x0, matrix products: 46.2 us -> none  [the longest x1 16.9 us: attend_rows(): jnp.einsum('qkgn,nkd->qkgd', weights, value_head_rows, precision=highest)]
    unnamed x1 -> x0, blocking collectives: 31.5 us -> none
    all_gather x1 -> x0, blocking collectives: 23 us -> none  [prefix(): pieces = jax.tree.map(lambda part: lax.all_gather(part, axis), value)]
    select_n x15 -> x0, other arithmetic: 17.6 us -> none  [hop(): jnp.where(position < mine, new, old)]
    reduce_scatter x2 -> x0, waiting for transfers between devices: 6.92 us -> none  [the longest x1 6.89 us: local(): lax.psum_scatter(grad_b, 'mp', scatter_dimension=0, tiled=True)]
  transfers between devices with their start and end apart: 6 -> 0, of which waited for: 5 -> 0; matrix products, arithmetic and copies ran while one was open for 12% -> 0% of each run, Pallas kernels for 0% -> 0%
where the time goes in v1:
time: 73.1 us; the launch traced here: 72.6 us
  Pallas kernels  64.9 us (89%)
  local copies, waits for them, and re-layouts  7.02 us (10%)
    pallas_call x1, Pallas kernels, local(): pl.pallas_call(functools.partial(kernel, planes, mp, c_scale), out_shape=...  64.9 us
    unnamed x16, local copies, waits for them, and re-layouts  7.02 us

profile of v1, /device:TPU:0, one launch (start us, length us, event | category | flops | bytes accessed | tf_op | source)
XLA Modules:
  0.0 72.6 jit_solution(1311657451449164583)
XLA Ops:
  0.6 0.0 copy-start.2
  0.6 0.8 %copy.10.ld_ref = f32[128,8]{1,0:T(8,128)S(1)} copy(f32[128,8]{0,1:T(8,128)} %param.13) | data formatting | bytes 8192 | tf_op args[6]
  1.5 0.0 copy-done.2
  1.5 0.0 copy-start
  1.5 0.9 %copy-done = bf16[128,1024]{1,0:T(8,128)(2,1)S(1)} copy-done((bf16[128,1024]{1,0:T(8,128)(2,1)S(1)}, bf16[128,1024]{1,0:T(8,128)(2,1)}, u32[]{:S(2)}) %copy-start) | copy-done | bytes 262168
  2.4 0.0 copy-start.1
  2.4 0.9 %copy-done.1 = bf16[128,1024]{1,0:T(8,128)(2,1)S(1)} copy-done((bf16[128,1024]{1,0:T(8,128)(2,1)S(1)}, bf16[128,1024]{1,0:T(8,128)(2,1)}, u32[]{:S(2)}) %copy-start.1) | copy-done | bytes 262168
  3.4 0.0 copy-start.3
  3.4 0.8 %copy-done.3 = bf16[128,128]{1,0:T(8,128)(2,1)S(1)} copy-done((bf16[128,128]{1,0:T(8,128)(2,1)S(1)}, bf16[128,128]{1,0:T(8,128)(2,1)}, u32[]{:S(2)}) %copy-start.3) | copy-done | bytes 32792
  4.1 0.0 copy-start.4
  4.1 0.8 %copy-done.4 = bf16[128,128]{1,0:T(8,128)(2,1)S(1)} copy-done((bf16[128,128]{1,0:T(8,128)(2,1)S(1)}, bf16[128,128]{1,0:T(8,128)(2,1)}, u32[]{:S(2)}) %copy-start.4) | copy-done | bytes 32792
  4.9 0.0 copy-start.5
  4.9 0.8 %copy-done.5 = bf16[128,128]{1,0:T(8,128)(2,1)S(1)} copy-done((bf16[128,128]{1,0:T(8,128)(2,1)S(1)}, bf16[128,128]{1,0:T(8,128)(2,1)}, u32[]{:S(2)}) %copy-start.5) | copy-done | bytes 32792
  5.6 64.9 %shard_map.94 = (f32[128,1024]{1,0:T(8,128)S(1)}, f32[64,128]{1,0:T(8,128)S(1)}, f32[64,128]{1,0:T(8,128)S(1)}) custom-call(bf16[128,1024]{1,0:T(8,128)(2,1)S(1)} %copy-done, bf16[128,128]{1,0:T(8,128)(2,1)S(1)} %copy-done.3, f32[128,128]{1,0:T(8,128)S(1)} %copy-done.2, bf16[128,1024]{1,0:T(8,128)(2,1)S(1)} %copy-done.1, bf16[128,128]{1,0:T(8,128)(2,1)S(1)} %copy-done.4, ...), custom_call_target="tpu_custom_call" | custom-call | flops 4000000000 | bytes 2000000 | tf_op jit(solution)/shard_map/pallas_call | solution.py:485
  70.6 0.8 %copy.14 = f32[128,1024]{1,0:T(8,128)} copy(f32[128,1024]{1,0:T(8,128)S(1)} %get-tuple-element.6) | data formatting | bytes 1048576
  71.4 0.6 copy.15
  72.0 0.6 copy.16
Async XLA Ops:
  0.6 0.8 %copy-start.2 = (f32[128,128]{1,0:T(8,128)S(1)}, f32[128,128]{1,0:T(8,128)}, u32[]{:S(2)}) copy-start(f32[128,128]{1,0:T(8,128)} %v_ref.1) | copy-start | bytes 196612
  1.5 0.9 %copy-start = (bf16[128,1024]{1,0:T(8,128)(2,1)S(1)}, bf16[128,1024]{1,0:T(8,128)(2,1)}, u32[]{:S(2)}) copy-start(bf16[128,1024]{1,0:T(8,128)(2,1)} %q_ref.1) | copy-start | bytes 786436
  2.4 0.9 %copy-start.1 = (bf16[128,1024]{1,0:T(8,128)(2,1)S(1)}, bf16[128,1024]{1,0:T(8,128)(2,1)}, u32[]{:S(2)}) copy-start(bf16[128,1024]{1,0:T(8,128)(2,1)} %x_ref.1) | copy-start | bytes 786436
  3.4 0.8 %copy-start.3 = (bf16[128,128]{1,0:T(8,128)(2,1)S(1)}, bf16[128,128]{1,0:T(8,128)(2,1)}, u32[]{:S(2)}) copy-start(bf16[128,128]{1,0:T(8,128)(2,1)} %k_ref.1) | copy-start | bytes 98308
  4.1 0.8 %copy-start.4 = (bf16[128,128]{1,0:T(8,128)(2,1)S(1)}, bf16[128,128]{1,0:T(8,128)(2,1)}, u32[]{:S(2)}) copy-start(bf16[128,128]{1,0:T(8,128)(2,1)} %b_ref.1) | copy-start | bytes 98308
  4.9 0.8 %copy-start.5 = (bf16[128,128]{1,0:T(8,128)(2,1)S(1)}, bf16[128,128]{1,0:T(8,128)(2,1)}, u32[]{:S(2)}) copy-start(bf16[128,128]{1,0:T(8,128)(2,1)} %c_ref.1) | copy-start | bytes 98308

commit v2 on v1

v2 whole, which is shorter than its diff:
```python
import functools
import math

import jax
import jax.numpy as jnp
from jax import lax
from jax.experimental import pallas as pl
from jax.experimental.pallas import tpu as pltpu
from jax.sharding import PartitionSpec as P

W = 128
HEADS = 8
PLANE = 4
MESH = pl.DeviceIdType.MESH
F32 = jnp.float32
BF = jnp.bfloat16
LOW = -1e30
PARTS = 4
HALF = 64


def dot(a, b):
    return lax.dot_general(a, b, (((1,), (0,)), ((), ())), preferred_element_type=F32)


def dot_nt(a, b):
    return lax.dot_general(a, b, (((1,), (1,)), ((), ())), preferred_element_type=F32)


def split(v):
    hi = v.astype(BF)
    return hi, (v - hi.astype(F32)).astype(BF)


def kernel(
    planes, mp, c_scale,
    q_hbm, k_hbm, v_hbm, x_hbm, b_hbm, c_hbm, ld_hbm,
    gx_ref, gb_ref, gc_ref,
    q_ref, k_ref, v_ref, x_ref, b_ref, c_ref, ld_ref,
    kv, cum, lsend, rs, zin, zout, run, decays, part, ag_out, s_in,
    lgsend, rsb, zinb, zoutb, agb_out, g_in,
    decay, mixt, ybuf, acc, top, den, qs, dbuf, gsum, mpb,
    in_s, kv_r, col_s, x_s, core_s, diag_s,
    rs_s, rs_r, z_s, z_r, ag_s, ag_r,
    rsb_s, rsb_r, zb_s, zb_r, agb_s, agb_r,
    mp_s, mp_r,
):
    s = lax.axis_index("seq")
    m = lax.axis_index("mp")
    z = s // PLANE
    r = s % PLANE
    base = z * PLANE
    core = r % 2
    rx = (r + 2) % PLANE
    rc = r + 1 - 2 * core
    rd = (rc + 2) % PLANE
    rows = W // mp
    levels = (planes - 1).bit_length()

    barrier = pltpu.get_barrier_semaphore()
    for k in range(1, PLANE):
        pl.semaphore_signal(
            barrier, inc=1, device_id=(base + (r + k) % PLANE, m), device_id_type=MESH
        )
    for k in range(1, mp):
        pl.semaphore_signal(barrier, inc=1, device_id=(s, (m + k) % mp), device_id_type=MESH)
    for k in range(1, planes):
        to = ((z + k) % planes) * PLANE + r
        pl.semaphore_signal(barrier, inc=1, device_id=(to, m), device_id_type=MESH)

    fetches = [
        pltpu.make_async_copy(src, dst, in_s.at[n])
        for n, (src, dst) in enumerate((
            (ld_hbm, ld_ref), (b_hbm, b_ref), (x_hbm, x_ref), (k_hbm, k_ref),
            (v_hbm, v_ref), (c_hbm, c_ref), (q_hbm, q_ref),
        ))
    ]
    for fetch in fetches:
        fetch.start()

    def remote(src, dst, send, recv, to):
        return pltpu.make_async_remote_copy(
            src_ref=src, dst_ref=dst, send_sem=send, recv_sem=recv,
            device_id=to, device_id_type=MESH,
        )

    def kv_copy(zp, rr, send, to):
        return remote(kv.at[zp, rr], kv.at[zp, rr], send, kv_r.at[zp, rr], to)

    def col(k):
        return kv_copy(z, r, col_s.at[k], (lax.rem(z + k, planes) * PLANE + r, m))

    def across(zp):
        return kv_copy(zp, r, x_s.at[zp], (base + rx, m))

    def chip(zp):
        return kv_copy(zp, r, core_s.at[zp], (base + rc, m))

    def diag(zp):
        return kv_copy(zp, rx, diag_s.at[zp], (base + rc, m))

    def arrived(zp, rr):
        kv_copy(zp, rr, x_s.at[zp], (base + rc, m)).wait_recv()

    def spread(zp):
        across(zp).start()
        chip(zp).start()

    at_row = lax.broadcasted_iota(jnp.int32, (W, W), 0)
    at_col = lax.broadcasted_iota(jnp.int32, (W, W), 1)
    tri = jnp.where(at_row <= at_col, 1.0, 0.0).astype(BF)
    fetches[0].wait()
    p0 = ld_ref[...].astype(BF)
    rest = ld_ref[...] - p0.astype(F32)
    p1 = rest.astype(BF)
    p2 = (rest - p1.astype(F32)).astype(BF)
    by_row = dot(p0, tri) + dot(p1, tri) + dot(p2, tri)
    for h in range(HEADS):
        cum[h] = jnp.broadcast_to(by_row[h : h + 1, :], (W, W)).T

    fetches[1].wait()
    fetches[2].wait()
    b = b_ref[...]
    b_t = b.astype(F32).T.astype(BF)

    pl.semaphore_wait(barrier, PLANE - 1 + mp - 1 + planes - 1)

    fetches[3].wait()
    fetches[4].wait()
    v_hi, v_lo = split(v_ref[...])
    kv[z, r, :, 0:W] = k_ref[...]
    kv[z, r, :, W : 2 * W] = v_hi
    kv[z, r, :, 2 * W : 3 * W] = v_lo
    for k in range(planes - 1, 0, -1):

        @pl.when(z + k < planes)
        def _():
            col(k).start()

    def head(ref, h):
        return ref[:, h * W : (h + 1) * W]

    def owner(k):
        return (r + k) % PLANE

    def to_owner(buf, land, send, recv, k, u):
        return remote(
            buf.at[owner(k), u], land.at[r, u], send.at[k, u], recv.at[r, u], (base + owner(k), m)
        )

    def from_peer(buf, land, send, recv, k, u):
        return remote(
            buf.at[owner(k), u], land.at[owner(k), u], send.at[k, u], recv.at[owner(k), u],
            (base + owner(k), m),
        )

    forth = (lsend, rs, rs_s, rs_r)
    back = (lgsend, rsb, rsb_s, rsb_r)
    give = (ag_out, s_in, ag_s, ag_r)
    give_back = (agb_out, g_in, agb_s, agb_r)
    far_first = (2, 3, 1)

    for g in range(2):
        for k in (2, 3, 1, 0):
            o = owner(k)
            h = 2 * o + g
            total = cum[h, W - 1 : W, :]
            ending = jnp.exp(total - cum[h])
            xh = x_ref[:, pl.ds(pl.multiple_of(h * W, W), W)]
            hi, lo = split(xh.astype(F32) * ending)
            state = dot(b_t, hi) + dot(b_t, lo)
            e = jnp.broadcast_to(jnp.exp(total), (8, W))
            to = lsend if k else rs
            for half in range(2):
                u = 2 * g + half
                to[o, u, 0:HALF, :] = state[half * HALF : (half + 1) * HALF]
                to[o, u, HALF : HALF + 8, :] = e
                if k:
                    to_owner(*forth, k, u).start()

    spread(z)

    fetches[5].wait()
    fetches[6].wait()
    c = c_ref[...]
    c_t = c.astype(F32).T.astype(BF)
    cb = dot_nt(c, b) * c_scale
    cb_t = dot_nt(b, c) * c_scale
    for h in range(HEADS):
        here = cum[h]
        other = here.T
        dec = jnp.exp(jnp.where(at_row >= at_col, here - other, LOW))
        dec_t = jnp.exp(jnp.where(at_row <= at_col, other - here, LOW))
        decay[h] = dec
        hi, lo = split(dec_t * cb_t)
        mixt[0, h] = hi
        mixt[1, h] = lo
        hi, lo = split(dec * cb)
        xh = head(x_ref, h)
        ybuf[h] = dot(hi, xh) + dot(lo, xh)
        qs[h] = head(q_ref, h)

    def pass_piece(i, carry):
        zp = z - 1 - i
        arrived(zp, r)
        spread(zp)
        return carry

    def plane_ready(zp):
        arrived(zp, rx)
        diag(zp).start()
        arrived(zp, rc)
        arrived(zp, rd)

    factor = math.log2(math.e) / math.sqrt(W)

    def attend(zp, first):
        keys = kv[zp, :, :, 0:W].reshape(PLANE * W, W)
        both = kv[zp, :, :, W : 3 * W].reshape(PLANE * W, 2 * W)
        v_top = kv[zp, :, :, W : 2 * W].reshape(PLANE * W, W)
        for h in range(HEADS):
            sc = dot_nt(qs[h], keys) * factor
            if first:
                t = lax.broadcasted_iota(jnp.int32, (W, PLANE * W), 0) + r * W
                u = lax.broadcasted_iota(jnp.int32, (W, PLANE * W), 1)
                sc = jnp.where(u <= t, sc, LOW)
            new = jnp.max(sc, axis=-1, keepdims=True)
            if not first:
                old = top[h][:, 0:1]
                new = jnp.maximum(old, new)
                scale = jnp.exp2(old - new)
            wt = jnp.exp2(sc - new)
            total = jnp.sum(wt, axis=-1, keepdims=True)
            hi, lo = split(wt)
            res = dot(hi, both)
            mix = res[:, 0:W] + res[:, W:] + dot(lo, v_top)
            if first:
                acc[h] = mix
                den[h] = jnp.broadcast_to(total, (W, W))
            else:
                acc[h] = acc[h] * scale + mix
                den[h] = den[h] * scale + total
            top[h] = jnp.broadcast_to(new, (W, W))

    plane_ready(z)
    lax.fori_loop(0, z, pass_piece, 0)
    attend(z, True)

    def attend_earlier(i, carry):
        zp = z - 1 - i
        plane_ready(zp)
        attend(zp, False)
        return carry

    def e_of(j, u):
        return rs[j, u, HALF : HALF + 1, :]

    def plane_terms(u, land, order, out):
        pre = None
        for j in order:
            if pre is not None:
                out[j, u] = pre
            local = land[j, u, 0:HALF, :]
            pre = local if pre is None else e_of(j, u) * pre + local
        part[u] = pre
        run[u] = jnp.zeros((HALF, W), F32)
        decays[u] = jnp.ones((8, W), F32)

    def hop(u, level, k, up, buf, land, send, recv):
        zt = lax.rem(z + (k if up else planes - k), planes)
        return remote(
            buf.at[u], land.at[level, u], send.at[k - 1, u], recv.at[level, u],
            (zt * PLANE + r, m),
        )

    def sends_at(zz, level):
        last = lax.rem(zz, 2 ** (level + 1)) == 2**level - 1
        return jnp.logical_and(last, zz < planes - 1)

    def send_level(u, level, zz, up, chain):
        buf = chain[0]

        @pl.when(sends_at(zz, level))
        def _():
            d = e_of(0, u) * e_of(1, u) * e_of(2, u) * e_of(3, u)
            buf[u, 0:HALF, :] = d * run[u] + part[u]
            buf[u, HALF : HALF + 8, :] = d * decays[u]
            for k in range(2**level, 0, -1):

                @pl.when(zz + k < planes)
                def _():
                    hop(u, level, k, up, *chain).start()

    def take_level(u, level, zz, up, chain):
        land = chain[1]

        @pl.when(lax.rem(zz // 2**level, 2) == 1)
        def _():
            hop(u, level, 1, up, *chain).wait_recv()
            run[u] = decays[u, 0:1, :] * land[level, u, 0:HALF, :] + run[u]
            decays[u] = decays[u] * land[level, u, HALF : HALF + 8, :]

    def hand_out(u, order, giving):
        out, land = giving[0], giving[1]
        came = run[u]
        coef = None
        for j in order:
            out[j, u] = came if coef is None else coef * came + out[j, u]
            coef = e_of(j, u) if coef is None else coef * e_of(j, u)
        for k in far_first:
            to_owner(*giving, k, u).start()
        land[r, u] = out[r, u]

    up_chain = (zout, zin, z_s, z_r)
    down_chain = (zoutb, zinb, zb_s, zb_r)
    order_up = tuple(range(PLANE))
    order_down = order_up[::-1]
    zb = planes - 1 - z

    for u in range(PARTS):
        for k in far_first:
            from_peer(*forth, k, u).wait_recv()
        plane_terms(u, rs, order_up, ag_out)
        send_level(u, 0, z, True, up_chain)

    before = jnp.where(jnp.logical_and(z % 2 == 1, z < planes - 1), 0, z)
    lax.fori_loop(0, before, attend_earlier, 0)

    for u in range(PARTS):
        for level in range(levels):
            if level:
                send_level(u, level, z, True, up_chain)
            take_level(u, level, z, True, up_chain)
        hand_out(u, order_up, give)

    lax.fori_loop(before, z, attend_earlier, 0)

    for g in range(2):
        for k in (0, 1, 2, 3):
            o = owner(k)
            h = 2 * o + g
            if k:
                for half in range(2):
                    from_peer(*give, k, 2 * g + half).wait_recv()
            rising = jnp.exp(cum[h])
            hi, lo = split(s_in[o, 2 * g : 2 * g + 2].reshape(W, W))
            inter = (dot(c, hi) + dot(c, lo)) * (rising * c_scale)
            d = ybuf[h] + inter - acc[h] / den[h]
            dbuf[h] = d
            hi, lo = split(d * rising)
            grad = (dot(c_t, hi) + dot(c_t, lo)) * c_scale
            to = lgsend if k else rsb
            for half in range(2):
                u = 2 * g + half
                to[o, u] = grad[half * HALF : (half + 1) * HALF]
                if k:
                    to_owner(*back, k, u).start()

    weighted = jnp.zeros((W, W), F32)
    grad_c = jnp.zeros((W, W), F32)
    for h in range(HEADS):
        d_hi, d_lo = split(dbuf[h])
        xh = head(x_ref, h)
        weighted += decay[h] * (dot_nt(d_hi, xh) + dot_nt(d_lo, xh))
        g = h % 2
        s_hi, s_lo = split(s_in[h // 2, 2 * g : 2 * g + 2].reshape(W, W))
        inter = dot_nt(d_hi, s_hi) + dot_nt(d_hi, s_lo) + dot_nt(d_lo, s_hi)
        grad_c += jnp.exp(cum[h]) * inter
        gx_ref[:, h * W : (h + 1) * W] = (
            dot(mixt[0, h], d_hi) + dot(mixt[0, h], d_lo) + dot(mixt[1, h], d_hi)
        )
    hi, lo = split(weighted)
    grad_c = (grad_c + dot(hi, b) + dot(lo, b)) * c_scale
    hi, lo = split(weighted.T)
    gsum[0] = (dot(hi, c) + dot(lo, c)) * c_scale
    gsum[1] = grad_c

    def mp_copy(k, which):
        to = (m + k) % mp
        return remote(
            gsum.at[which, pl.ds(pl.multiple_of(to * rows, 8), rows)],
            mpb.at[k - 1, which],
            mp_s.at[k - 1, which], mp_r.at[k - 1, which], (s, to),
        )

    for k in range(1, mp):
        mp_copy(k, 1).start()

    for u in range(PARTS):
        for k in far_first:
            from_peer(*back, k, u).wait_recv()
        plane_terms(u, rsb, order_down, agb_out)
        send_level(u, 0, zb, False, down_chain)

    for u in range(PARTS):
        for level in range(levels):
            if level:
                send_level(u, level, zb, False, down_chain)
            take_level(u, level, zb, False, down_chain)
        hand_out(u, order_down, give_back)

    grad_b = gsum[0]
    for g in range(2):
        for k in (0, 1, 2, 3):
            o = owner(k)
            h = 2 * o + g
            if k:
                for half in range(2):
                    from_peer(*give_back, k, 2 * g + half).wait_recv()
            ending = jnp.exp(cum[h, W - 1 : W, :] - cum[h])
            hi, lo = split(g_in[o, 2 * g : 2 * g + 2].reshape(W, W))
            lanes = pl.ds(pl.multiple_of(h * W, W), W)
            gx_ref[:, lanes] += (dot(b, hi) + dot(b, lo)) * ending
            xh = x_ref[:, lanes]
            grad_b += (dot_nt(xh, hi) + dot_nt(xh, lo)) * ending
    gsum[0] = grad_b
    for k in range(1, mp):
        mp_copy(k, 0).start()

    for k in far_first:
        for u in range(PARTS):
            for route in (forth, back, give, give_back):
                to_owner(*route, k, u).wait_send()
    for k in range(1, planes):

        @pl.when(z + k < planes)
        def _():
            col(k).wait_send()

    def sent(zp, carry):
        across(zp).wait_send()
        chip(zp).wait_send()
        diag(zp).wait_send()
        return carry

    lax.fori_loop(0, z + 1, sent, 0)

    for zz, up, chain in ((z, True, up_chain), (zb, False, down_chain)):
        for level in range(levels):

            @pl.when(sends_at(zz, level))
            def _():
                for k in range(2**level, 0, -1):

                    @pl.when(zz + k < planes)
                    def _():
                        for u in range(PARTS):
                            hop(u, level, k, up, *chain).wait_send()

    own = pl.ds(pl.multiple_of(m * rows, 8), rows)
    for which, out in ((1, gc_ref), (0, gb_ref)):
        total = gsum[which, own]
        for k in range(1, mp):
            mp_copy(k, which).wait_recv()
            total += mpb[k - 1, which]
        out[...] = total
    for which in range(2):
        for k in range(1, mp):
            mp_copy(k, which).wait_send()


def local(queries, keys, values, inputs_x, in_b, in_c, log_decay):
    tokens = queries.shape[0]
    seq = lax.axis_size("seq")
    mp = lax.axis_size("mp")
    planes = seq // PLANE
    c_scale = 0.5 / math.sqrt(W * tokens * seq)
    dma = pltpu.SemaphoreType.DMA
    levels = max((planes - 1).bit_length(), 1)
    reach = max(planes - 1, 1)
    msg = (PARTS, HALF + 8, W)
    plain = (PARTS, HALF, W)
    scratch = [
        pltpu.VMEM((tokens, HEADS * W), BF),
        pltpu.VMEM((tokens, W), BF),
        pltpu.VMEM((tokens, W), F32),
        pltpu.VMEM((tokens, HEADS * W), BF),
        pltpu.VMEM((tokens, W), BF),
        pltpu.VMEM((tokens, W), BF),
        pltpu.VMEM((HEADS, tokens), F32),
        pltpu.VMEM((planes, PLANE, W, 3 * W), BF),
        pltpu.VMEM((HEADS, W, W), F32),
        pltpu.VMEM((PLANE,) + msg, F32),
        pltpu.VMEM((PLANE,) + msg, F32),
        pltpu.VMEM((levels,) + msg, F32),
        pltpu.VMEM(msg, F32),
        pltpu.VMEM(plain, F32),
        pltpu.VMEM((PARTS, 8, W), F32),
        pltpu.VMEM(plain, F32),
        pltpu.VMEM((PLANE,) + plain, F32),
        pltpu.VMEM((PLANE,) + plain, F32),
        pltpu.VMEM((PLANE,) + plain, F32),
        pltpu.VMEM((PLANE,) + plain, F32),
        pltpu.VMEM((levels,) + msg, F32),
        pltpu.VMEM(msg, F32),
        pltpu.VMEM((PLANE,) + plain, F32),
        pltpu.VMEM((PLANE,) + plain, F32),
        pltpu.VMEM((HEADS, W, W), F32),
        pltpu.VMEM((2, HEADS, W, W), BF),
        pltpu.VMEM((HEADS, W, W), F32),
        pltpu.VMEM((HEADS, W, W), F32),
        pltpu.VMEM((HEADS, W, W), F32),
        pltpu.VMEM((HEADS, W, W), F32),
        pltpu.VMEM((HEADS, W, W), BF),
        pltpu.VMEM((HEADS, W, W), F32),
        pltpu.VMEM((2, W, W), F32),
        pltpu.VMEM((max(mp - 1, 1), 2, W // mp, W), F32),
        dma((7,)),
        dma((planes, PLANE)), dma((planes,)), dma((planes,)), dma((planes,)), dma((planes,)),
        dma((PLANE, PARTS)), dma((PLANE, PARTS)), dma((reach, PARTS)), dma((levels, PARTS)),
        dma((PLANE, PARTS)), dma((PLANE, PARTS)),
        dma((PLANE, PARTS)), dma((PLANE, PARTS)), dma((reach, PARTS)), dma((levels, PARTS)),
        dma((PLANE, PARTS)), dma((PLANE, PARTS)),
        dma((max(mp - 1, 1), 2)), dma((max(mp - 1, 1), 2)),
    ]
    vmem = pl.BlockSpec(memory_space=pltpu.VMEM)
    return pl.pallas_call(
        functools.partial(kernel, planes, mp, c_scale),
        out_shape=(
            jax.ShapeDtypeStruct((tokens, HEADS * W), F32),
            jax.ShapeDtypeStruct((tokens // mp, W), F32),
            jax.ShapeDtypeStruct((tokens // mp, W), F32),
        ),
        in_specs=[pl.BlockSpec(memory_space=pl.ANY)] * 7,
        out_specs=(vmem,) * 3,
        scratch_shapes=scratch,
        compiler_params=pltpu.CompilerParams(
            collective_id=0, has_side_effects=True, vmem_limit_bytes=56 << 20
        ),
        cost_estimate=pl.CostEstimate(
            flops=4_000_000_000, bytes_accessed=2_000_000, transcendentals=2_500_000
        ),
    )(queries, keys, values, inputs_x, in_b, in_c, log_decay.T)


def solution(mesh):
    in_specs = (
        P("seq", "mp"), P("seq", "mp"), P("seq", "mp"), P("seq", "mp"),
        P("seq", None), P("seq", None), P("seq", "mp"),
    )
    out_specs = (P("seq", "mp"), P(("seq", "mp"), None), P(("seq", "mp"), None))
    return jax.shard_map(local, mesh=mesh, in_specs=in_specs, out_specs=out_specs, check_vma=False)
```

time: 73.1 us -> 67.4 us (0.922)
  local copies, waits for them, and re-layouts: 7.02 us -> 3.28 us
  Pallas kernels: 64.9 us -> 63.2 us
    unnamed x16 -> x7, local copies, waits for them, and re-layouts: 7.02 us -> 3.28 us
    pallas_call x1, Pallas kernels: 64.9 us -> 63.2 us  [local(): pl.pallas_call(functools.partial(kernel, planes, mp, c_scale), out_shape=...]
where the time goes in v2:
time: 67.4 us; the launch traced here: 67.2 us
  Pallas kernels  63.2 us (94%)
  local copies, waits for them, and re-layouts  3.28 us (5%)
    pallas_call x1, Pallas kernels, local(): pl.pallas_call(functools.partial(kernel, planes, mp, c_scale), out_shape=...  63.2 us
    unnamed x7, local copies, waits for them, and re-layouts  3.28 us

profile of v2, /device:TPU:0, one launch (start us, length us, event | category | flops | bytes accessed | tf_op | source)
XLA Modules:
  0.0 67.2 jit_solution(14730843719853485657)
XLA Ops:
  0.6 63.2 %shard_map.94 = (f32[128,1024]{1,0:T(8,128)}, f32[64,128]{1,0:T(8,128)}, f32[64,128]{1,0:T(8,128)}) custom-call(bf16[128,1024]{1,0:T(8,128)(2,1)} %q_hbm.1, bf16[128,128]{1,0:T(8,128)(2,1)} %k_hbm.1, f32[128,128]{1,0:T(8,128)} %v_hbm.1, bf16[128,1024]{1,0:T(8,128)(2,1)} %x_hbm.1, bf16[128,128]{1,0:T(8,128)(2,1)} %b_hbm.1, bf16[128,128]{1,0:T(8,128)(2,1)} %c_hbm.1, ...), custom_call_target="tpu_custom_call" | custom-call | flops 4000000000 | bytes 2000000 | tf_op jit(solution)/shard_map/pallas_call | solution.py:517
  63.9 0.0 copy-start.1
  63.9 1.9 %copy.13 = f32[128,1024]{1,0:T(8,128)} copy(f32[128,1024]{1,0:T(8,128)} %get-tuple-element.6) | data formatting | bytes 1048576
  65.8 0.0 copy-done.1
  65.8 0.0 copy-start
  65.8 0.6 copy.14
  66.4 0.2 copy-done
  66.6 0.6 copy.15
Async XLA Ops:
  63.9 1.9 %copy-start.1 = (f32[64,128]{1,0:T(8,128)S(1)}, f32[64,128]{1,0:T(8,128)}, u32[]{:S(2)}) copy-start(f32[64,128]{1,0:T(8,128)} %get-tuple-element.7) | copy-start | bytes 98308
  65.8 0.8 %copy-start = (f32[64,128]{1,0:T(8,128)S(1)}, f32[64,128]{1,0:T(8,128)}, u32[]{:S(2)}) copy-start(f32[64,128]{1,0:T(8,128)} %get-tuple-element.8) | copy-start | bytes 98308

commit v3 on v2

--- a/solution.py
+++ b/solution.py
@@ -17,6 +17,7 @@
 LOW = -1e30
 PARTS = 4
 HALF = 64
+BLOCK = 4
 
 
 def dot(a, b):
@@ -25,6 +26,14 @@
 
 def dot_nt(a, b):
     return lax.dot_general(a, b, (((1,), (1,)), ((), ())), preferred_element_type=F32)
+
+
+def side(*parts):
+    return jnp.concatenate(parts, axis=1)
+
+
+def stack(*parts):
+    return jnp.concatenate(parts, axis=0)
 
 
 def split(v):
@@ -160,23 +169,22 @@
     give_back = (agb_out, g_in, agb_s, agb_r)
     far_first = (2, 3, 1)
 
+    bb_t = side(b_t, b_t)
     for g in range(2):
-        for k in (2, 3, 1, 0):
-            o = owner(k)
+        for o in range(PLANE):
             h = 2 * o + g
             total = cum[h, W - 1 : W, :]
             ending = jnp.exp(total - cum[h])
-            xh = x_ref[:, pl.ds(pl.multiple_of(h * W, W), W)]
-            hi, lo = split(xh.astype(F32) * ending)
-            state = dot(b_t, hi) + dot(b_t, lo)
+            state = dot(bb_t, stack(*split(head(x_ref, h).astype(F32) * ending)))
             e = jnp.broadcast_to(jnp.exp(total), (8, W))
-            to = lsend if k else rs
             for half in range(2):
                 u = 2 * g + half
-                to[o, u, 0:HALF, :] = state[half * HALF : (half + 1) * HALF]
-                to[o, u, HALF : HALF + 8, :] = e
-                if k:
-                    to_owner(*forth, k, u).start()
+                lsend[o, u, 0:HALF, :] = state[half * HALF : (half + 1) * HALF]
+                lsend[o, u, HALF : HALF + 8, :] = e
+        for u in (2 * g, 2 * g + 1):
+            for k in far_first:
+                to_owner(*forth, k, u).start()
+            rs[r, u] = lsend[r, u]
 
     spread(z)
 
@@ -188,17 +196,15 @@
     cb_t = dot_nt(b, c) * c_scale
     for h in range(HEADS):
         here = cum[h]
-        other = here.T
+        other = jnp.broadcast_to(by_row[h : h + 1, :], (W, W))
         dec = jnp.exp(jnp.where(at_row >= at_col, here - other, LOW))
         dec_t = jnp.exp(jnp.where(at_row <= at_col, other - here, LOW))
         decay[h] = dec
         hi, lo = split(dec_t * cb_t)
-        mixt[0, h] = hi
-        mixt[1, h] = lo
-        hi, lo = split(dec * cb)
+        mixt[h] = side(hi, hi, lo)
         xh = head(x_ref, h)
-        ybuf[h] = dot(hi, xh) + dot(lo, xh)
-        qs[h] = head(q_ref, h)
+        ybuf[h] = dot(side(*split(dec * cb)), stack(xh, xh))
+        qs[h * W : (h + 1) * W, :] = head(q_ref, h)
 
     def pass_piece(i, carry):
         zp = z - 1 - i
@@ -218,29 +224,33 @@
         keys = kv[zp, :, :, 0:W].reshape(PLANE * W, W)
         both = kv[zp, :, :, W : 3 * W].reshape(PLANE * W, 2 * W)
         v_top = kv[zp, :, :, W : 2 * W].reshape(PLANE * W, W)
-        for h in range(HEADS):
-            sc = dot_nt(qs[h], keys) * factor
+        block = BLOCK * W
+        for at in range(0, HEADS * W, block):
+            sc = dot_nt(qs[at : at + block, :], keys) * factor
             if first:
-                t = lax.broadcasted_iota(jnp.int32, (W, PLANE * W), 0) + r * W
-                u = lax.broadcasted_iota(jnp.int32, (W, PLANE * W), 1)
+                t = lax.broadcasted_iota(jnp.int32, (block, PLANE * W), 0) % W + r * W
+                u = lax.broadcasted_iota(jnp.int32, (block, PLANE * W), 1)
                 sc = jnp.where(u <= t, sc, LOW)
-            new = jnp.max(sc, axis=-1, keepdims=True)
+            new = jnp.broadcast_to(jnp.max(sc, axis=-1, keepdims=True), (block, W))
             if not first:
-                old = top[h][:, 0:1]
+                old = top[at : at + block, :]
                 new = jnp.maximum(old, new)
                 scale = jnp.exp2(old - new)
-            wt = jnp.exp2(sc - new)
-            total = jnp.sum(wt, axis=-1, keepdims=True)
-            hi, lo = split(wt)
-            res = dot(hi, both)
-            mix = res[:, 0:W] + res[:, W:] + dot(lo, v_top)
-            if first:
-                acc[h] = mix
-                den[h] = jnp.broadcast_to(total, (W, W))
-            else:
-                acc[h] = acc[h] * scale + mix
-                den[h] = den[h] * scale + total
-            top[h] = jnp.broadcast_to(new, (W, W))
+            his, los, total = [], [], None
+            for j in range(PLANE):
+                wt = jnp.exp2(sc[:, j * W : (j + 1) * W] - new)
+                total = wt if total is None else total + wt
+                hi, lo = split(wt)
+                his.append(hi)
+                los.append(lo)
+            res = dot(side(*his), both)
+            mix = res[:, 0:W] + res[:, W:] + dot(side(*los), v_top)
+            if not first:
+                mix = acc[at : at + block, :] * scale + mix
+                total = den[at : at + block, :] * scale + total
+            acc[at : at + block, :] = mix
+            den[at : at + block, :] = total
+            top[at : at + block, :] = new
 
     plane_ready(z)
     lax.fori_loop(0, z, pass_piece, 0)
@@ -335,44 +345,41 @@
 
     lax.fori_loop(before, z, attend_earlier, 0)
 
+    cc = side(c, c)
+    cc_t = side(c_t, c_t)
     for g in range(2):
-        for k in (0, 1, 2, 3):
-            o = owner(k)
+        for k in far_first:
+            for half in range(2):
+                from_peer(*give, k, 2 * g + half).wait_recv()
+        for o in range(PLANE):
             h = 2 * o + g
-            if k:
-                for half in range(2):
-                    from_peer(*give, k, 2 * g + half).wait_recv()
+            at = h * W
             rising = jnp.exp(cum[h])
-            hi, lo = split(s_in[o, 2 * g : 2 * g + 2].reshape(W, W))
-            inter = (dot(c, hi) + dot(c, lo)) * (rising * c_scale)
-            d = ybuf[h] + inter - acc[h] / den[h]
+            inter = dot(cc, stack(*split(s_in[o, 2 * g : 2 * g + 2].reshape(W, W))))
+            under = jnp.sum(den[at : at + W, :], axis=-1, keepdims=True)
+            d = ybuf[h] + inter * (rising * c_scale) - acc[at : at + W, :] / under
             dbuf[h] = d
-            hi, lo = split(d * rising)
-            grad = (dot(c_t, hi) + dot(c_t, lo)) * c_scale
-            to = lgsend if k else rsb
+            grad = dot(cc_t, stack(*split(d * rising))) * c_scale
             for half in range(2):
-                u = 2 * g + half
-                to[o, u] = grad[half * HALF : (half + 1) * HALF]
-                if k:
-                    to_owner(*back, k, u).start()
+                lgsend[o, 2 * g + half] = grad[half * HALF : (half + 1) * HALF]
+        for u in (2 * g, 2 * g + 1):
+            for k in far_first:
+                to_owner(*back, k, u).start()
+            rsb[r, u] = lgsend[r, u]
 
     weighted = jnp.zeros((W, W), F32)
     grad_c = jnp.zeros((W, W), F32)
     for h in range(HEADS):
         d_hi, d_lo = split(dbuf[h])
         xh = head(x_ref, h)
-        weighted += decay[h] * (dot_nt(d_hi, xh) + dot_nt(d_lo, xh))
+        weighted += decay[h] * dot_nt(side(d_hi, d_lo), side(xh, xh))
         g = h % 2
         s_hi, s_lo = split(s_in[h // 2, 2 * g : 2 * g + 2].reshape(W, W))
-        inter = dot_nt(d_hi, s_hi) + dot_nt(d_hi, s_lo) + dot_nt(d_lo, s_hi)
+        inter = dot_nt(side(d_hi, d_hi, d_lo), side(s_hi, s_lo, s_hi))
         grad_c += jnp.exp(cum[h]) * inter
-        gx_ref[:, h * W : (h + 1) * W] = (
-            dot(mixt[0, h], d_hi) + dot(mixt[0, h], d_lo) + dot(mixt[1, h], d_hi)
-        )
-    hi, lo = split(weighted)
-    grad_c = (grad_c + dot(hi, b) + dot(lo, b)) * c_scale
-    hi, lo = split(weighted.T)
-    gsum[0] = (dot(hi, c) + dot(lo, c)) * c_scale
+        gx_ref[:, h * W : (h + 1) * W] = dot(mixt[h], stack(d_hi, d_lo, d_hi))
+    grad_c = (grad_c + dot(side(*split(weighted)), stack(b, b))) * c_scale
+    gsum[0] = dot(side(*split(weighted.T)), stack(c, c)) * c_scale
     gsum[1] = grad_c
 
     def mp_copy(k, which):
@@ -399,20 +406,19 @@
             take_level(u, level, zb, False, down_chain)
         hand_out(u, order_down, give_back)
 
+    bb = side(b, b)
     grad_b = gsum[0]
     for g in range(2):
-        for k in (0, 1, 2, 3):
-            o = owner(k)
+        for k in far_first:
+            for half in range(2):
+                from_peer(*give_back, k, 2 * g + half).wait_recv()
+        for o in range(PLANE):
             h = 2 * o + g
-            if k:
-                for half in range(2):
-                    from_peer(*give_back, k, 2 * g + half).wait_recv()
             ending = jnp.exp(cum[h, W - 1 : W, :] - cum[h])
             hi, lo = split(g_in[o, 2 * g : 2 * g + 2].reshape(W, W))
-            lanes = pl.ds(pl.multiple_of(h * W, W), W)
-            gx_ref[:, lanes] += (dot(b, hi) + dot(b, lo)) * ending
-            xh = x_ref[:, lanes]
-            grad_b += (dot_nt(xh, hi) + dot_nt(xh, lo)) * ending
+            gx_ref[:, h * W : (h + 1) * W] += dot(bb, stack(hi, lo)) * ending
+            xh = head(x_ref, h)
+            grad_b += dot_nt(side(xh, xh), side(hi, lo)) * ending
     gsum[0] = grad_b
     for k in range(1, mp):
         mp_copy(k, 0).start()
@@ -496,12 +502,12 @@
         pltpu.VMEM((PLANE,) + plain, F32),
         pltpu.VMEM((PLANE,) + plain, F32),
         pltpu.VMEM((HEADS, W, W), F32),
-        pltpu.VMEM((2, HEADS, W, W), BF),
+        pltpu.VMEM((HEADS, W, 3 * W), BF),
         pltpu.VMEM((HEADS, W, W), F32),
-        pltpu.VMEM((HEADS, W, W), F32),
-        pltpu.VMEM((HEADS, W, W), F32),
-        pltpu.VMEM((HEADS, W, W), F32),
-        pltpu.VMEM((HEADS, W, W), BF),
+        pltpu.VMEM((HEADS * W, W), F32),
+        pltpu.VMEM((HEADS * W, W), F32),
+        pltpu.VMEM((HEADS * W, W), F32),
+        pltpu.VMEM((HEADS * W, W), BF),
         pltpu.VMEM((HEADS, W, W), F32),
         pltpu.VMEM((2, W, W), F32),
         pltpu.VMEM((max(mp - 1, 1), 2, W // mp, W), F32),
@@ -525,7 +531,7 @@
         out_specs=(vmem,) * 3,
         scratch_shapes=scratch,
         compiler_params=pltpu.CompilerParams(
-            collective_id=0, has_side_effects=True, vmem_limit_bytes=56 << 20
+            collective_id=0, has_side_effects=True, vmem_limit_bytes=40 << 20
         ),
         cost_estimate=pl.CostEstimate(
             flops=4_000_000_000, bytes_accessed=2_000_000, transcendentals=2_500_000

time: 67.4 us -> 65.3 us (0.969)
  Pallas kernels: 63.2 us -> 56.5 us
  local copies, waits for them, and re-layouts: 3.28 us -> 7.71 us
    pallas_call x1, Pallas kernels: 63.2 us -> 56.5 us  [local(): pl.pallas_call(functools.partial(kernel, planes, mp, c_scale), out_shape=...]
    unnamed x7 -> x17, local copies, waits for them, and re-layouts: 3.28 us -> 7.71 us
where the time goes in v3:
time: 65.3 us; the launch traced here: 64.8 us
  Pallas kernels  56.5 us (87%)
  local copies, waits for them, and re-layouts  7.71 us (12%)
  between operations  0.66 us (1%)
    pallas_call x1, Pallas kernels, local(): pl.pallas_call(functools.partial(kernel, planes, mp, c_scale), out_shape=...  56.5 us
    unnamed x17, local copies, waits for them, and re-layouts  7.71 us

profile of v3, /device:TPU:0, one launch (start us, length us, event | category | flops | bytes accessed | tf_op | source)
XLA Modules:
  0.0 64.8 jit_solution(9963538635099979348)
XLA Ops:
  0.6 0.0 copy-start
  0.6 0.9 %copy-done = bf16[128,1024]{1,0:T(8,128)(2,1)S(1)} copy-done((bf16[128,1024]{1,0:T(8,128)(2,1)S(1)}, bf16[128,1024]{1,0:T(8,128)(2,1)}, u32[]{:S(2)}) %copy-start) | copy-done | bytes 262168
  1.6 0.0 copy-start.1
  1.6 0.9 %copy-done.1 = bf16[128,1024]{1,0:T(8,128)(2,1)S(1)} copy-done((bf16[128,1024]{1,0:T(8,128)(2,1)S(1)}, bf16[128,1024]{1,0:T(8,128)(2,1)}, u32[]{:S(2)}) %copy-start.1) | copy-done | bytes 262168
  2.5 0.0 copy-start.2
  2.5 0.8 %copy-done.2 = f32[128,128]{1,0:T(8,128)S(1)} copy-done((f32[128,128]{1,0:T(8,128)S(1)}, f32[128,128]{1,0:T(8,128)}, u32[]{:S(2)}) %copy-start.2) | copy-done | bytes 65560
  3.4 0.0 copy-start.3
  3.4 0.8 %copy-done.3 = bf16[128,128]{1,0:T(8,128)(2,1)S(1)} copy-done((bf16[128,128]{1,0:T(8,128)(2,1)S(1)}, bf16[128,128]{1,0:T(8,128)(2,1)}, u32[]{:S(2)}) %copy-start.3) | copy-done | bytes 32792
  4.1 0.0 copy-start.4
  4.1 0.8 %copy-done.4 = bf16[128,128]{1,0:T(8,128)(2,1)S(1)} copy-done((bf16[128,128]{1,0:T(8,128)(2,1)S(1)}, bf16[128,128]{1,0:T(8,128)(2,1)}, u32[]{:S(2)}) %copy-start.4) | copy-done | bytes 32792
  4.9 0.0 copy-start.5
  4.9 0.8 %copy-done.5 = bf16[128,128]{1,0:T(8,128)(2,1)S(1)} copy-done((bf16[128,128]{1,0:T(8,128)(2,1)S(1)}, bf16[128,128]{1,0:T(8,128)(2,1)}, u32[]{:S(2)}) %copy-start.5) | copy-done | bytes 32792
  5.6 0.0 copy-start.6
  5.7 0.7 %copy-done.6 = f32[128,8]{0,1:T(8,128)S(1)} copy-done((f32[128,8]{0,1:T(8,128)S(1)}, f32[128,8]{0,1:T(8,128)}, u32[]{:S(2)}) %copy-start.6) | copy-done | bytes 4120
  6.3 56.5 %shard_map.94 = (f32[128,1024]{1,0:T(8,128)S(1)}, f32[64,128]{1,0:T(8,128)S(1)}, f32[64,128]{1,0:T(8,128)S(1)}) custom-call(bf16[128,1024]{1,0:T(8,128)(2,1)S(1)} %copy-done, bf16[128,128]{1,0:T(8,128)(2,1)S(1)} %copy-done.3, f32[128,128]{1,0:T(8,128)S(1)} %copy-done.2, bf16[128,1024]{1,0:T(8,128)(2,1)S(1)} %copy-done.1, bf16[128,128]{1,0:T(8,128)(2,1)S(1)} %copy-done.4, ...), custom_call_target="tpu_custom_call" | custom-call | flops 4000000000 | bytes 2000000 | tf_op jit(solution)/shard_map/pallas_call | solution.py:523
  62.8 0.8 %copy.13 = f32[128,1024]{1,0:T(8,128)} copy(f32[128,1024]{1,0:T(8,128)S(1)} %get-tuple-element.6) | data formatting | bytes 1048576
  63.6 0.6 copy.14
  64.2 0.6 copy.15
Async XLA Ops:
  0.6 1.0 %copy-start = (bf16[128,1024]{1,0:T(8,128)(2,1)S(1)}, bf16[128,1024]{1,0:T(8,128)(2,1)}, u32[]{:S(2)}) copy-start(bf16[128,1024]{1,0:T(8,128)(2,1)} %q_hbm.1) | copy-start | bytes 786436
  1.6 0.9 %copy-start.1 = (bf16[128,1024]{1,0:T(8,128)(2,1)S(1)}, bf16[128,1024]{1,0:T(8,128)(2,1)}, u32[]{:S(2)}) copy-start(bf16[128,1024]{1,0:T(8,128)(2,1)} %x_hbm.1) | copy-start | bytes 786436
  2.5 0.8 %copy-start.2 = (f32[128,128]{1,0:T(8,128)S(1)}, f32[128,128]{1,0:T(8,128)}, u32[]{:S(2)}) copy-start(f32[128,128]{1,0:T(8,128)} %v_hbm.1) | copy-start | bytes 196612
  3.4 0.8 %copy-start.3 = (bf16[128,128]{1,0:T(8,128)(2,1)S(1)}, bf16[128,128]{1,0:T(8,128)(2,1)}, u32[]{:S(2)}) copy-start(bf16[128,128]{1,0:T(8,128)(2,1)} %k_hbm.1) | copy-start | bytes 98308
  4.1 0.8 %copy-start.4 = (bf16[128,128]{1,0:T(8,128)(2,1)S(1)}, bf16[128,128]{1,0:T(8,128)(2,1)}, u32[]{:S(2)}) copy-start(bf16[128,128]{1,0:T(8,128)(2,1)} %b_hbm.1) | copy-start | bytes 98308
  4.9 0.8 %copy-start.5 = (bf16[128,128]{1,0:T(8,128)(2,1)S(1)}, bf16[128,128]{1,0:T(8,128)(2,1)}, u32[]{:S(2)}) copy-start(bf16[128,128]{1,0:T(8,128)(2,1)} %c_hbm.1) | copy-start | bytes 98308
  5.6 0.7 %copy-start.6 = (f32[128,8]{0,1:T(8,128)S(1)}, f32[128,8]{0,1:T(8,128)}, u32[]{:S(2)}) copy-start(f32[128,8]{0,1:T(8,128)} %param.13) | copy-start | bytes 12292

commit v4 on v3

--- a/solution.py
+++ b/solution.py
@@ -333,7 +333,7 @@
         plane_terms(u, rs, order_up, ag_out)
         send_level(u, 0, z, True, up_chain)
 
-    before = jnp.where(jnp.logical_and(z % 2 == 1, z < planes - 1), 0, z)
+    before = jnp.maximum(z - 2, 0)
     lax.fori_loop(0, before, attend_earlier, 0)
 
     for u in range(PARTS):
@@ -531,7 +531,7 @@
         out_specs=(vmem,) * 3,
         scratch_shapes=scratch,
         compiler_params=pltpu.CompilerParams(
-            collective_id=0, has_side_effects=True, vmem_limit_bytes=40 << 20
+            collective_id=0, has_side_effects=True, vmem_limit_bytes=56 << 20
         ),
         cost_estimate=pl.CostEstimate(
             flops=4_000_000_000, bytes_accessed=2_000_000, transcendentals=2_500_000

time: 65.3 us -> 63.4 us (0.971)
  local copies, waits for them, and re-layouts: 7.71 us -> 3.28 us
  Pallas kernels: 56.5 us -> 59.2 us
    unnamed x17 -> x7, local copies, waits for them, and re-layouts: 7.71 us -> 3.28 us
    pallas_call x1, Pallas kernels: 56.5 us -> 59.2 us  [local(): pl.pallas_call(functools.partial(kernel, planes, mp, c_scale), out_shape=...]
where the time goes in v4:
time: 63.4 us; the launch traced here: 63.2 us
  Pallas kernels  59.2 us (93%)
  local copies, waits for them, and re-layouts  3.28 us (5%)
  between operations  0.65 us (1%)
    pallas_call x1, Pallas kernels, local(): pl.pallas_call(functools.partial(kernel, planes, mp, c_scale), out_shape=...  59.2 us
    unnamed x7, local copies, waits for them, and re-layouts  3.28 us

profile of v4, /device:TPU:0, one launch (start us, length us, event | category | flops | bytes accessed | tf_op | source)
XLA Modules:
  0.0 63.2 jit_solution(12126021053533758653)
XLA Ops:
  0.6 59.2 %shard_map.94 = (f32[128,1024]{1,0:T(8,128)}, f32[64,128]{1,0:T(8,128)}, f32[64,128]{1,0:T(8,128)}) custom-call(bf16[128,1024]{1,0:T(8,128)(2,1)} %q_hbm.1, bf16[128,128]{1,0:T(8,128)(2,1)} %k_hbm.1, f32[128,128]{1,0:T(8,128)} %v_hbm.1, bf16[128,1024]{1,0:T(8,128)(2,1)} %x_hbm.1, bf16[128,128]{1,0:T(8,128)(2,1)} %b_hbm.1, bf16[128,128]{1,0:T(8,128)(2,1)} %c_hbm.1, ...), custom_call_target="tpu_custom_call" | custom-call | flops 4000000000 | bytes 2000000 | tf_op jit(solution)/shard_map/pallas_call | solution.py:523
  59.9 0.0 copy-start.1
  59.9 1.9 %copy.13 = f32[128,1024]{1,0:T(8,128)} copy(f32[128,1024]{1,0:T(8,128)} %get-tuple-element.6) | data formatting | bytes 1048576
  61.8 0.0 copy-done.1
  61.8 0.0 copy-start
  61.8 0.6 copy.14
  62.4 0.2 copy-done
  62.6 0.6 copy.15
Async XLA Ops:
  59.9 1.9 %copy-start.1 = (f32[64,128]{1,0:T(8,128)S(1)}, f32[64,128]{1,0:T(8,128)}, u32[]{:S(2)}) copy-start(f32[64,128]{1,0:T(8,128)} %get-tuple-element.7) | copy-start | bytes 98308
  61.8 0.8 %copy-start = (f32[64,128]{1,0:T(8,128)S(1)}, f32[64,128]{1,0:T(8,128)}, u32[]{:S(2)}) copy-start(f32[64,128]{1,0:T(8,128)} %get-tuple-element.8) | copy-start | bytes 98308

commit v5 on v4

--- a/solution.py
+++ b/solution.py
@@ -333,7 +333,7 @@
         plane_terms(u, rs, order_up, ag_out)
         send_level(u, 0, z, True, up_chain)
 
-    before = jnp.maximum(z - 2, 0)
+    before = jnp.maximum(z - 1, 0)
     lax.fori_loop(0, before, attend_earlier, 0)
 
     for u in range(PARTS):

time: 63.4 us -> 61.1 us (0.964)
  Pallas kernels: 59.2 us -> 56.9 us
    pallas_call x1, Pallas kernels: 59.2 us -> 56.9 us  [local(): pl.pallas_call(functools.partial(kernel, planes, mp, c_scale), out_shape=...]
where the time goes in v5:
time: 61.1 us; the launch traced here: 60.9 us
  Pallas kernels  56.9 us (93%)
  local copies, waits for them, and re-layouts  3.28 us (5%)
  between operations  0.65 us (1%)
    pallas_call x1, Pallas kernels, local(): pl.pallas_call(functools.partial(kernel, planes, mp, c_scale), out_shape=...  56.9 us
    unnamed x7, local copies, waits for them, and re-layouts  3.28 us

profile of v5, /device:TPU:0, one launch (start us, length us, event | category | flops | bytes accessed | tf_op | source)
XLA Modules:
  0.0 60.9 jit_solution(15917372829245924169)
XLA Ops:
  0.6 56.9 %shard_map.94 = (f32[128,1024]{1,0:T(8,128)}, f32[64,128]{1,0:T(8,128)}, f32[64,128]{1,0:T(8,128)}) custom-call(bf16[128,1024]{1,0:T(8,128)(2,1)} %q_hbm.1, bf16[128,128]{1,0:T(8,128)(2,1)} %k_hbm.1, f32[128,128]{1,0:T(8,128)} %v_hbm.1, bf16[128,1024]{1,0:T(8,128)(2,1)} %x_hbm.1, bf16[128,128]{1,0:T(8,128)(2,1)} %b_hbm.1, bf16[128,128]{1,0:T(8,128)(2,1)} %c_hbm.1, ...), custom_call_target="tpu_custom_call" | custom-call | flops 4000000000 | bytes 2000000 | tf_op jit(solution)/shard_map/pallas_call | solution.py:523
  57.6 0.0 copy-start.1
  57.6 1.9 %copy.13 = f32[128,1024]{1,0:T(8,128)} copy(f32[128,1024]{1,0:T(8,128)} %get-tuple-element.6) | data formatting | bytes 1048576
  59.5 0.0 copy-done.1
  59.5 0.0 copy-start
  59.5 0.6 %copy.14 = f32[64,128]{1,0:T(8,128)} copy(f32[64,128]{1,0:T(8,128)S(1)} %copy-done.1) | data formatting | bytes 65536
  60.1 0.2 copy-done
  60.3 0.6 %copy.15 = f32[64,128]{1,0:T(8,128)} copy(f32[64,128]{1,0:T(8,128)S(1)} %copy-done) | data formatting | bytes 65536
Async XLA Ops:
  57.6 1.9 %copy-start.1 = (f32[64,128]{1,0:T(8,128)S(1)}, f32[64,128]{1,0:T(8,128)}, u32[]{:S(2)}) copy-start(f32[64,128]{1,0:T(8,128)} %get-tuple-element.7) | copy-start | bytes 98308
  59.5 0.8 %copy-start = (f32[64,128]{1,0:T(8,128)S(1)}, f32[64,128]{1,0:T(8,128)}, u32[]{:S(2)}) copy-start(f32[64,128]{1,0:T(8,128)} %get-tuple-element.8) | copy-start | bytes 98308
